TPU v7x, 32 devices: a whole 2x2x4 slice. The times are simulated.
32 devices in a mesh: dp: 8 (over z, y), expert: 4 (over x, core).
Axes of the slice: x: 2, y: 2, z: 4, core: 2. Of those that a mesh axis runs over, the one named last changes fastest.
Arguments:
- local_grads: bfloat16 [4, 8, 1024, 3584], P('expert', 'dp')
- momentum: float32 [4, 1024, 3584], P('expert', None, 'dp'), may hold values from -6 to 6
Outputs:
- new_momentum: float32 [4, 1024, 3584], P('expert', None, 'dp')
- update: float32 [4, 1024, 3584], P('expert', None, 'dp')
All inputs are finite; a program needn't handle non-finite values.
Results may differ from a plain program's by a relative error of at most 0.0003.
Values sent between devices are 32-bit elements; how exact they have to be, the bound alone decides.
No kernel may reach another device: no remote copies, remote signals or barrier semaphores. Data moves between devices by JAX's collectives and lax.ppermute only.
A program may use at most 128 MiB of HBM per device.

v0:
```python
import math

import jax
import jax.numpy as jnp
from jax import lax
from jax.sharding import PartitionSpec as P

HID = 1024
WID = 3584
ITERS = 3


first_coef = 3.4445
second_coef = -4.775
third_coef = 2.0315
momentum_decay = 0.95


def precise(left, right):
    return jnp.dot(left, right, precision=lax.Precision.HIGHEST, preferred_element_type=jnp.float32)


def body(local_grads, momentum):
    grads = lax.psum_scatter(
        local_grads[0, 0].astype(jnp.float32), "dp", scatter_dimension=1, tiled=True
    )
    count = HID * WID * lax.axis_size("expert")
    total_sq = lax.psum(jnp.sum(grads * grads), ("dp", "expert"))
    root_mean = jnp.sqrt(total_sq / count + 1e-06)
    factor = jnp.minimum(1.0, 1.0 / root_mean)
    clipped = factor * grads
    new_momentum = momentum_decay * momentum[0] + clipped
    iterate = clipped + momentum_decay * new_momentum
    for number in range(ITERS):
        partial_value = precise(iterate, iterate.T)
        gram = lax.psum(partial_value, "dp")
        if number == 0:
            norm_scale = jnp.sqrt(jnp.trace(gram)) + 1e-07
            iterate = iterate / norm_scale
            gram = gram / (norm_scale * norm_scale)
        product = precise(gram, iterate)
        iterate = first_coef * iterate + second_coef * product + third_coef * precise(gram, product)
    update = iterate * (0.2 * math.sqrt(max(HID, WID)))
    return (new_momentum[None], update[None])


def solution(mesh):
    return jax.shard_map(
        body,
        mesh=mesh,
        in_specs=(P("expert", "dp", None, None), P("expert", None, "dp")),
        out_specs=(P("expert", None, "dp"), P("expert", None, "dp")),
        check_vma=False,
    )
```

profile of v0, /device:TPU:0, one launch (start us, length us, event | category | flops | bytes accessed | tf_op | source)
XLA Modules:
  0.0 866.4 jit_solution(10076177830157491438)
XLA Ops:
  7.2 0.0 reduce-scatter.2.cloned.1.call-start
  7.2 10.4 %copy.4 = bf16[1,1,1024,3584]{2,3,1,0:T(8,128)(2,1)} copy(bf16[1,1,1024,3584]{3,2,1,0:T(8,128)(2,1)} %param.2) | data formatting | bytes 14680064 | tf_op args[0]
  17.6 10.2 %bitcast_convert_fusion = f32[1024,3584]{0,1:T(8,128)} fusion(bf16[1,1,1024,3584]{2,3,1,0:T(8,128)(2,1)} %copy.4), kind=kLoop, calls=%fused_computation | loop fusion | flops 3670016 | bytes 22020096 | tf_op jit(solution)/shard_map/convert_element_type | solution.py:25
  27.8 0.0 reduce-scatter.2.cloned.1.call-update
  27.8 0.0 all-reduce.4.cloned.1.call-start
  27.9 239.3 %reduce-scatter.2.cloned.1.call-done = f32[1024,448]{0,1:T(8,128)} async-done(((f32[1024,3584]{0,1:T(8,128)}), f32[1024,448]{0,1:T(8,128)}) %reduce-scatter.2.cloned.1.call-update) | async-done | bytes 1835024 | tf_op jit(solution)/shard_map/reduce_scatter | solution.py:24
  267.2 2.6 multiply_reduce_fusion
  269.8 39.6 %psum.28 = f32[]{:T(128)} all-reduce(f32[]{:T(128)} %multiply_reduce_fusion), channel_id=1, replica_groups=mesh['dp'=8,'expert'=4] {'dp','expert'}, use_global_device_ids=true, to_apply=%region_2.0 | all-reduce | flops 1 | bytes 8 | tf_op jit(solution)/shard_map/psum | solution.py:28
  310.0 3.9 multiply_add_fusion.2
  313.9 8.5 fusion.3
  322.4 0.0 all-reduce.4.cloned.1.call-update
  322.5 0.2 all-reduce.6.cloned.1.call-start
  322.7 156.2 %all-reduce.4.cloned.1.call-done = f32[1024,1024]{1,0:T(8,128)} async-done(((f32[1024,1024]{1,0:T(8,128)}), f32[1024,1024]{1,0:T(8,128)}) %all-reduce.4.cloned.1.call-update) | async-done | bytes 4194320 | tf_op jit(solution)/shard_map/psum | solution.py:36
  478.9 2.9 select_reduce_fusion
  482.5 0.0 copy-done.1
  482.5 0.0 copy-start.4
  482.5 8.6 fusion.1
  491.1 0.0 copy-done.4
  491.1 7.7 multiply_add_fusion.1
  498.8 0.0 copy-start
  498.8 8.7 %fusion.4 = f32[1024,1024]{1,0:T(8,128)} fusion(f32[1024,448]{0,1:T(8,128)S(1)} %multiply_add_fusion.1), kind=kOutput, calls=%fused_computation.15 | convolution fusion | flops 5637144576 | bytes 6029312 | tf_op jit(solution)/shard_map/dot_general | solution.py:20
  507.6 0.0 all-reduce.6.cloned.1.call-update
  507.6 0.0 all-reduce.8.cloned.1.call-start
  507.6 155.4 %all-reduce.6.cloned.1.call-done = f32[1024,1024]{1,0:T(8,128)} async-done(((f32[1024,1024]{1,0:T(8,128)}), f32[1024,1024]{1,0:T(8,128)}) %all-reduce.6.cloned.1.call-update) | async-done | bytes 4194320 | tf_op jit(solution)/shard_map/psum | solution.py:36
  663.0 0.0 copy-done
  663.0 8.4 fusion.5
  671.5 7.7 multiply_add_fusion
  679.1 8.8 %fusion.6 = f32[1024,1024]{1,0:T(8,128)} fusion(f32[1024,448]{0,1:T(8,128)S(1)} %multiply_add_fusion), kind=kOutput, calls=%fused_computation.17 | convolution fusion | flops 5637144576 | bytes 6029312 | tf_op jit(solution)/shard_map/dot_general | solution.py:20
  687.9 0.0 all-reduce.8.cloned.1.call-update
  687.9 155.5 %all-reduce.8.cloned.1.call-done = f32[1024,1024]{1,0:T(8,128)} async-done(((f32[1024,1024]{1,0:T(8,128)}), f32[1024,1024]{1,0:T(8,128)}) %all-reduce.8.cloned.1.call-update) | async-done | bytes 4194320 | tf_op jit(solution)/shard_map/psum | solution.py:36
  843.4 8.8 %fusion.7 = f32[1024,448]{0,1:T(8,128)S(1)} fusion(f32[1024,1024]{1,0:T(8,128)} %all-reduce.8.cloned.1.call-done, f32[1024,448]{0,1:T(8,128)S(1)} %multiply_add_fusion), kind=kOutput, calls=%fused_computation.18 | convolution fusion | flops 5637144576 | bytes 7864320 | tf_op jit(solution)/shard_map/dot_general | solution.py:20
  852.2 7.4 multiply_bitcast_fusion
  (5 shorter events, 0.0 us)
Async XLA Ops:
  7.2 260.0 %reduce-scatter.2.cloned.1.call-start = ((), (), s32[]{:S(2)}) async-start(), calls=%async_computation.1 | async-start | bytes 16515072 | tf_op jit(solution)/shard_map/reduce_scatter | solution.py:24
  27.8 451.1 %all-reduce.4.cloned.1.call-start = ((), (), s32[]{:S(2)}) async-start(), calls=%async_computation.2 | async-start | bytes 8388608 | tf_op jit(solution)/shard_map/psum | solution.py:36
  313.9 168.6 %copy-start.1 = (f32[1024,448]{0,1:T(8,128)}, f32[1024,448]{0,1:T(8,128)S(1)}, u32[]{:S(2)}) copy-start(f32[1024,448]{0,1:T(8,128)S(1)} %get-tuple-element.2) | copy-start | bytes 5505028
  322.5 340.6 %all-reduce.6.cloned.1.call-start = ((), (), s32[]{:S(2)}) async-start(), calls=%async_computation.3 | async-start | bytes 8388608 | tf_op jit(solution)/shard_map/psum | solution.py:36
  482.5 8.6 copy-start.4
  498.8 164.2 %copy-start = (f32[1024,448]{0,1:T(8,128)}, f32[1024,448]{0,1:T(8,128)S(1)}, u32[]{:S(2)}) copy-start(f32[1024,448]{0,1:T(8,128)S(1)} %multiply_add_fusion.1) | copy-start | bytes 5505028
  507.6 335.8 %all-reduce.8.cloned.1.call-start = ((), (), s32[]{:S(2)}) async-start(), calls=%async_computation.4 | async-start | bytes 8388608 | tf_op jit(solution)/shard_map/psum | solution.py:36
  663.0 8.4 copy-start.2
  843.4 8.9 %copy-start.3 = (f32[1024,1024]{1,0:T(8,128)S(1)}, f32[1024,1024]{1,0:T(8,128)}, u32[]{:S(2)}) copy-start(f32[1024,1024]{1,0:T(8,128)} %all-reduce.8.cloned.1.call-done) | copy-start | bytes 12582916
Sparse Core Ops, SparseCore 0:
  27.9 239.1 reduce-scatter.1
  322.6 156.2 all-reduce.3
  507.7 155.2 all-reduce.5
  688.0 155.2 all-reduce.7
where the time goes:
time: 872 us; the launch traced here: 866 us
  waiting for transfers between devices  706 us (81%)
  matrix products  74.6 us (9%)
  blocking collectives  39.6 us (5%)
  other arithmetic  19.6 us (2%)
  between operations  15.4 us (2%)
  local copies, waits for them, and re-layouts  10.5 us (1%)
    psum x3, waiting for transfers between devices, body(): gram = lax.psum(partial_value, 'dp')  467 us
    reduce_scatter x1, waiting for transfers between devices, body(): lax.psum_scatter(local_grads[0, 0].astype(jnp.float32), 'dp', scatter_dim...  239 us
    dot_general x9, matrix products, precise(): jnp.dot(left, right, precision=lax.Precision.HIGHEST, preferred_element_t...  74.6 us
    psum x1, blocking collectives, body(): total_sq = lax.psum(jnp.sum(grads * grads), ('dp', 'expert'))  39.6 us
  transfers between devices with their start and end apart: 4, of which 4 were waited for; matrix products, arithmetic and copies ran while one was open for 0% of the time, Pallas kernels for 0%

commit v1 on v0

v1 whole, which is shorter than its diff:
```python
import math

import jax
import jax.numpy as jnp
from jax import lax
from jax.sharding import PartitionSpec as P

ITERS = 3

first_coef = 3.4445
second_coef = -4.775
third_coef = 2.0315
momentum_decay = 0.95


def product(left, right):
    return jnp.dot(left, right, precision=lax.Precision.HIGH, preferred_element_type=jnp.float32)


def body(local_grads, momentum):
    hid, wid = local_grads.shape[2:]
    grads = lax.psum_scatter(
        local_grads[0, 0].astype(jnp.float32), "dp", scatter_dimension=1, tiled=True
    )
    count = hid * wid * lax.axis_size("expert")
    total_sq = lax.psum(jnp.sum(grads * grads), ("dp", "expert"))
    root_mean = jnp.sqrt(total_sq / count + 1e-06)
    factor = jnp.minimum(1.0, 1.0 / root_mean)
    clipped = factor * grads
    new_momentum = momentum_decay * momentum[0] + clipped
    blend = clipped + momentum_decay * new_momentum
    gram = lax.psum(product(blend, blend.T), "dp")
    norm = jnp.sqrt(jnp.trace(gram)) + 1e-07
    iterate = blend / norm
    gram = gram / (norm * norm)
    eye = jnp.eye(hid, dtype=jnp.float32)
    for number in range(ITERS):
        poly = first_coef * eye + second_coef * gram + third_coef * product(gram, gram)
        iterate = product(poly, iterate)
        if number < ITERS - 1:
            gram = product(product(gram, poly), poly)
    update = iterate * (0.2 * math.sqrt(max(hid, wid)))
    return (new_momentum[None], update[None])


def solution(mesh):
    return jax.shard_map(
        body,
        mesh=mesh,
        in_specs=(P("expert", "dp", None, None), P("expert", None, "dp")),
        out_specs=(P("expert", None, "dp"), P("expert", None, "dp")),
        check_vma=False,
    )
```

time: 872 us -> 560 us (0.64)
  waiting for transfers between devices: 706 us -> 393 us
    psum x3 -> x1, waiting for transfers between devices: 467 us -> 153 us  [body(): gram = lax.psum(product(blend, blend.T), 'dp')]
    dot_general x9 -> x11, matrix products: 74.6 us -> 74.1 us  [product(): jnp.dot(left, right, precision=lax.Precision.HIGH, preferred_element_type...]
  transfers between devices with their start and end apart: 4 -> 2, of which waited for: 4 -> 2; matrix products, arithmetic and copies ran while one was open for 0% -> 1% of each run, Pallas kernels for 0% -> 0%
where the time goes in v1:
time: 560 us; the launch traced here: 552 us
  waiting for transfers between devices  393 us (70%)
  matrix products  74.1 us (13%)
  blocking collectives  39.6 us (7%)
  other arithmetic  18.8 us (3%)
  between operations  15.9 us (3%)
  local copies, waits for them, and re-layouts  10.4 us (2%)
    reduce_scatter x1, waiting for transfers between devices, body(): lax.psum_scatter(local_grads[0, 0].astype(jnp.float32), 'dp', scatter_dim...  239 us
    psum x1, waiting for transfers between devices, body(): gram = lax.psum(product(blend, blend.T), 'dp')  153 us
    dot_general x11, matrix products, product(): jnp.dot(left, right, precision=lax.Precision.HIGH, preferred_element_type...  74.1 us
    psum x1, blocking collectives, body(): total_sq = lax.psum(jnp.sum(grads * grads), ('dp', 'expert'))  39.6 us
  transfers between devices with their start and end apart: 2, of which 2 were waited for; matrix products, arithmetic and copies ran while one was open for 1% of the time, Pallas kernels for 0%

profile of v1, /device:TPU:0, one launch (start us, length us, event | category | flops | bytes accessed | tf_op | source)
XLA Modules:
  0.0 551.6 jit_solution(13869378690419919354)
XLA Ops:
  7.2 0.0 reduce-scatter.2.cloned.1.call-start
  7.2 10.4 %copy.4 = bf16[1,1,1024,3584]{2,3,1,0:T(8,128)(2,1)} copy(bf16[1,1,1024,3584]{3,2,1,0:T(8,128)(2,1)} %param.2) | data formatting | bytes 14680064 | tf_op args[0]
  17.6 10.2 %bitcast_convert_fusion = f32[1024,3584]{0,1:T(8,128)} fusion(bf16[1,1,1024,3584]{2,3,1,0:T(8,128)(2,1)} %copy.4), kind=kLoop, calls=%fused_computation | loop fusion | flops 3670016 | bytes 22020096 | tf_op jit(solution)/shard_map/convert_element_type | solution.py:23
  27.8 0.0 reduce-scatter.2.cloned.1.call-update
  27.8 0.0 all-reduce.2.cloned.1.call-start
  27.9 239.3 %reduce-scatter.2.cloned.1.call-done = f32[1024,448]{0,1:T(8,128)} async-done(((f32[1024,3584]{0,1:T(8,128)}), f32[1024,448]{0,1:T(8,128)}) %reduce-scatter.2.cloned.1.call-update) | async-done | bytes 1835024 | tf_op jit(solution)/shard_map/reduce_scatter | solution.py:22
  267.2 2.6 multiply_reduce_fusion
  269.8 39.6 %psum.14 = f32[]{:T(128)} all-reduce(f32[]{:T(128)} %multiply_reduce_fusion), channel_id=1, replica_groups=mesh['dp'=8,'expert'=4] {'dp','expert'}, use_global_device_ids=true, to_apply=%region_2.0 | all-reduce | flops 1 | bytes 8 | tf_op jit(solution)/shard_map/psum | solution.py:26
  310.0 0.0 copy-start
  310.0 8.9 %fusion.52 = f32[1024,1024]{1,0:T(8,128)} fusion(f32[1024,448]{0,1:T(8,128)} %reduce-scatter.2.cloned.1.call-done, f32[1,1024,448]{1,2,0:T(8,128)} %param.3, f32[]{:T(128)S(6)} %min.3), kind=kOutput, calls=%fused_computation.54 | convolution fusion | flops 2820866048 | bytes 7864324 | tf_op jit(solution)/shard_map/dot_general | solution.py:17
  318.9 0.0 all-reduce.2.cloned.1.call-update
  319.0 0.0 copy-done
  319.0 3.1 fusion.50
  322.1 153.3 %all-reduce.2.cloned.1.call-done = f32[1024,1024]{1,0:T(8,128)} async-done(((f32[1024,1024]{1,0:T(8,128)}), f32[1024,1024]{1,0:T(8,128)}) %all-reduce.2.cloned.1.call-update) | async-done | bytes 4194320 | tf_op jit(solution)/shard_map/psum | solution.py:32
  475.4 2.9 select_reduce_fusion
  479.1 0.0 copy-start.2
  479.1 10.9 %fusion.83 = f32[1024,1024]{1,0:T(8,128)S(1)} fusion(f32[1024,1024]{1,0:T(8,128)} %all-reduce.2.cloned.1.call-done, f32[]{:T(128)S(6)} %mul.61), kind=kOutput, calls=%fused_computation.85 | convolution fusion | flops 6443499520 | bytes 8388612 | tf_op jit(solution)/shard_map/dot_general | solution.py:17
  489.9 0.0 copy-done.2
  490.0 6.9 %fusion.17 = f32[1024,1024]{1,0:T(8,128)S(1)} fusion(f32[1024,1024]{1,0:T(8,128)S(1)} %fusion.83, f32[1024,1024]{1,0:T(8,128)S(1)} %copy-done.2, f32[]{:T(128)S(6)} %mul.61), kind=kOutput, calls=%fused_computation.17 | convolution fusion | flops 6450839552 | bytes 12582916 | tf_op jit(solution)/shard_map/dot_general | solution.py:17
  496.9 7.3 %fusion.15 = f32[1024,1024]{1,0:T(8,128)S(1)} fusion(f32[1024,1024]{1,0:T(8,128)S(1)} %fusion.17, f32[1024,1024]{1,0:T(8,128)S(1)} %fusion.83, f32[1024,1024]{1,0:T(8,128)S(1)} %copy-done.2, f32[]{:T(128)S(6)} %mul.61), kind=kOutput, calls=%fused_computation.16 | convolution fusion | flops 6449790976 | bytes 16777220 | tf_op jit(solution)/shard_map/dot_general | solution.py:17
  504.2 7.0 %fusion.84 = f32[1024,1024]{1,0:T(8,128)S(1)} fusion(f32[1024,1024]{1,0:T(8,128)S(1)} %fusion.15), kind=kOutput, calls=%fused_computation.86 | convolution fusion | flops 6442450944 | bytes 8388608 | tf_op jit(solution)/shard_map/dot_general | solution.py:17
  511.2 0.0 copy-start.1
  511.2 7.1 %fusion.11 = f32[1024,1024]{1,0:T(8,128)S(1)} fusion(f32[1024,1024]{1,0:T(8,128)S(1)} %fusion.15, f32[1024,1024]{1,0:T(8,128)S(1)} %fusion.84), kind=kOutput, calls=%fused_computation.14 | convolution fusion | flops 6448742400 | bytes 12582912 | tf_op jit(solution)/shard_map/dot_general | solution.py:17
  518.4 0.0 copy-done.1
  518.4 3.7 fusion.13
  522.1 3.6 fusion.7
  525.7 7.2 %fusion.9 = f32[1024,1024]{1,0:T(8,128)S(1)} fusion(f32[1024,1024]{1,0:T(8,128)S(1)} %fusion.11, f32[1024,1024]{1,0:T(8,128)S(1)} %fusion.84, f32[1024,1024]{1,0:T(8,128)S(1)} %fusion.15), kind=kOutput, calls=%fused_computation.13 | convolution fusion | flops 6448742400 | bytes 16777216 | tf_op jit(solution)/shard_map/dot_general | solution.py:17
  532.9 6.9 %fusion.85 = f32[1024,1024]{1,0:T(8,128)S(1)} fusion(f32[1024,1024]{1,0:T(8,128)S(1)} %fusion.9), kind=kOutput, calls=%fused_computation.87 | convolution fusion | flops 6442450944 | bytes 8388608 | tf_op jit(solution)/shard_map/dot_general | solution.py:17
  539.8 4.6 multiply_bitcast_fusion
Async XLA Ops:
  7.2 260.0 %reduce-scatter.2.cloned.1.call-start = ((), (), s32[]{:S(2)}) async-start(), calls=%async_computation.1 | async-start | bytes 16515072 | tf_op jit(solution)/shard_map/reduce_scatter | solution.py:22
  27.8 447.6 %all-reduce.2.cloned.1.call-start = ((), (), s32[]{:S(2)}) async-start(), calls=%async_computation.2 | async-start | bytes 8388608 | tf_op jit(solution)/shard_map/psum | solution.py:32
  310.0 9.0 %copy-start = (f32[1024,448]{0,1:T(8,128)S(1)}, f32[1024,448]{0,1:T(8,128)}, u32[]{:S(2)}) copy-start(f32[1024,448]{0,1:T(8,128)} %reduce-scatter.2.cloned.1.call-done) | copy-start | bytes 5505028
  479.1 10.9 %copy-start.2 = (f32[1024,1024]{1,0:T(8,128)S(1)}, f32[1024,1024]{1,0:T(8,128)}, u32[]{:S(2)}) copy-start(f32[1024,1024]{1,0:T(8,128)} %all-reduce.2.cloned.1.call-done) | copy-start | bytes 12582916
  511.2 7.1 %copy-start.1 = (f32[1,1024,448]{1,2,0:T(8,128)S(1)}, f32[1,1024,448]{1,2,0:T(8,128)}, u32[]{:S(2)}) copy-start(f32[1,1024,448]{1,2,0:T(8,128)} %param.3) | copy-start | bytes 5505028
Sparse Core Ops, SparseCore 0:
  27.9 239.1 reduce-scatter.1
  319.1 156.2 all-reduce.1

commit v2 on v1

--- a/solution.py
+++ b/solution.py
@@ -6,6 +6,8 @@
 from jax.sharding import PartitionSpec as P
 
 ITERS = 3
+STREAMS = 4
+FOLD = 128
 
 first_coef = 3.4445
 second_coef = -4.775
@@ -17,19 +19,94 @@
     return jnp.dot(left, right, precision=lax.Precision.HIGH, preferred_element_type=jnp.float32)
 
 
+def ring_order(size):
+    return list(range(0, size, 2)) + list(range(1, size, 2))[::-1]
+
+
+class Ring:
+    def __init__(self, axis):
+        self.axis = axis
+        self.size = lax.axis_size(axis)
+        self.order = ring_order(self.size)
+        cycle = self.order + self.order
+        table = [cycle[cycle.index(index):][:self.size] for index in range(self.size)]
+        self.owners = jnp.array(table, jnp.int32)[lax.axis_index(axis)]
+
+    def owner(self, offset):
+        return self.owners[offset % self.size]
+
+    def send(self, value, way):
+        pairs = [(self.order[p], self.order[(p + way) % self.size]) for p in range(self.size)]
+        return lax.ppermute(value, self.axis, pairs)
+
+
+def ring_sum_scatter(ring, terms):
+    ways = [1 if k % 2 == 0 else -1 for k in range(len(terms))]
+
+    def local(k, offset):
+        return lax.dynamic_index_in_dim(terms[k], ring.owner(offset), 0, keepdims=False).astype(jnp.float32)
+
+    held = [local(k, -way) for k, way in enumerate(ways)]
+    for step in range(ring.size - 1):
+        for k, way in enumerate(ways):
+            held[k] = ring.send(held[k], way) + local(k, -way * (step + 2))
+    return held
+
+
+def direct_sum(value, axis):
+    size = lax.axis_size(axis)
+    total = value
+    for shift in range(1, size):
+        total = total + lax.ppermute(value, axis, [(p, (p + shift) % size) for p in range(size)])
+    return total
+
+
+def fold(gram):
+    size = gram.shape[0]
+    parts = size // FOLD
+    rows = []
+    for p in range(parts // 2):
+        q = parts - 1 - p
+        rows.append(jnp.concatenate(
+            [gram[p * FOLD:(p + 1) * FOLD, p * FOLD:], gram[q * FOLD:(q + 1) * FOLD, q * FOLD:]], axis=1
+        ))
+    return jnp.concatenate(rows, axis=0)
+
+
+def unfold(packed, size):
+    parts = size // FOLD
+    blocks = {}
+    for p in range(parts // 2):
+        q = parts - 1 - p
+        row = packed[p * FOLD:(p + 1) * FOLD]
+        for c in range(p, parts):
+            blocks[p, c] = row[:, (c - p) * FOLD:(c - p + 1) * FOLD]
+        for c in range(q, parts):
+            at = parts - p + c - q
+            blocks[q, c] = row[:, at * FOLD:(at + 1) * FOLD]
+    return jnp.concatenate([
+        jnp.concatenate([blocks[r, c] if c >= r else blocks[c, r].T for c in range(parts)], axis=1)
+        for r in range(parts)
+    ], axis=0)
+
+
 def body(local_grads, momentum):
     hid, wid = local_grads.shape[2:]
-    grads = lax.psum_scatter(
-        local_grads[0, 0].astype(jnp.float32), "dp", scatter_dimension=1, tiled=True
-    )
+    ring = Ring("dp")
+    rows = hid // STREAMS
+    terms = [
+        local_grads[0, 0, k * rows:(k + 1) * rows].reshape(rows, ring.size, wid // ring.size).transpose(1, 0, 2)
+        for k in range(STREAMS)
+    ]
+    grads = jnp.concatenate(ring_sum_scatter(ring, terms), axis=0)
     count = hid * wid * lax.axis_size("expert")
-    total_sq = lax.psum(jnp.sum(grads * grads), ("dp", "expert"))
+    total_sq = direct_sum(direct_sum(jnp.sum(grads * grads).reshape(1), "dp"), "expert")[0]
     root_mean = jnp.sqrt(total_sq / count + 1e-06)
     factor = jnp.minimum(1.0, 1.0 / root_mean)
     clipped = factor * grads
     new_momentum = momentum_decay * momentum[0] + clipped
     blend = clipped + momentum_decay * new_momentum
-    gram = lax.psum(product(blend, blend.T), "dp")
+    gram = unfold(lax.psum(fold(product(blend, blend.T)), "dp"), hid)
     norm = jnp.sqrt(jnp.trace(gram)) + 1e-07
     iterate = blend / norm
     gram = gram / (norm * norm)

time: 560 us -> 490 us (0.88)
  waiting for transfers between devices: 393 us -> 212 us
  local copies, waits for them, and re-layouts: 10.4 us -> 78.7 us
  starting transfers between devices: 0.08 us -> 47.2 us
  blocking collectives: 39.6 us -> 0 us
  between operations: 15.9 us -> 37.4 us
  matrix products: 74.1 us -> 89 us
    reduce_scatter x1 -> x0, waiting for transfers between devices: 239 us -> none  [body(): lax.psum_scatter(local_grads[0, 0].astype(jnp.float32), 'dp', scatter_dim...]
    ppermute x0 -> x38, waiting for transfers between devices: none -> 106 us  [the longest x28 89.6 us: send(): return lax.ppermute(value, self.axis, pairs)]
    psum x1, waiting for transfers between devices: 153 us -> 105 us  [body(): gram = unfold(lax.psum(fold(product(blend, blend.T)), 'dp'), hid)]
    ppermute x0 -> x38, starting transfers between devices: none -> 47.2 us  [the longest x28 33.4 us: send(): return lax.ppermute(value, self.axis, pairs)]
    psum x1 -> x0, blocking collectives: 39.6 us -> none  [body(): total_sq = lax.psum(jnp.sum(grads * grads), ('dp', 'expert'))]
    unnamed x7 -> x136, local copies, waits for them, and re-layouts: 10.4 us -> 42.3 us
    slice x0 -> x19, local copies, waits for them, and re-layouts: none -> 24.9 us  [the longest x5 19.4 us: body(): local_grads[0, 0, k * rows:(k + 1) * rows]]
    dot_general x11, matrix products: 74.1 us -> 89 us  [product(): jnp.dot(left, right, precision=lax.Precision.HIGH, preferred_element_type...]
  transfers between devices with their start and end apart: 2 -> 39, of which waited for: 2 -> 23; matrix products, arithmetic and copies ran while one was open for 1% -> 4% of each run, Pallas kernels for 0% -> 0%
where the time goes in v2:
time: 490 us; the launch traced here: 481 us
  waiting for transfers between devices  212 us (43%)
  matrix products  89 us (18%)
  local copies, waits for them, and re-layouts  78.7 us (16%)
  starting transfers between devices  47.2 us (10%)
  between operations  37.4 us (8%)
  other arithmetic  17.6 us (4%)
    psum x1, waiting for transfers between devices, body(): gram = unfold(lax.psum(fold(product(blend, blend.T)), 'dp'), hid)  105 us
    ppermute x28, waiting for transfers between devices, send(): return lax.ppermute(value, self.axis, pairs)  89.6 us
    dot_general x11, matrix products, product(): jnp.dot(left, right, precision=lax.Precision.HIGH, preferred_element_type...  89 us
    unnamed x136, local copies, waits for them, and re-layouts  42.3 us
    ppermute x28, starting transfers between devices, send(): return lax.ppermute(value, self.axis, pairs)  33.4 us
    slice x5, local copies, waits for them, and re-layouts, body(): local_grads[0, 0, k * rows:(k + 1) * rows]  19.4 us
    ppermute x10, waiting for transfers between devices, direct_sum(): lax.ppermute(value, axis, [(p, (p + shift) % size) for p in range(size)])  16.8 us
    ppermute x10, starting transfers between devices, direct_sum(): lax.ppermute(value, axis, [(p, (p + shift) % size) for p in range(size)])  13.8 us
  transfers between devices with their start and end apart: 39, of which 23 were waited for; matrix products, arithmetic and copies ran while one was open for 4% of the time, Pallas kernels for 0%

profile of v2, /device:TPU:0, one launch (start us, length us, event | category | flops | bytes accessed | tf_op | source)
XLA Modules:
  0.0 481.4 jit_solution(12204070091490570603)
XLA Ops:
  9.8 5.8 %fusion.68 = (bf16[1,1,256,3584]{3,2,1,0:T(8,128)(2,1)}, bf16[1,1,256,3584]{3,2,1,0:T(8,128)(2,1)}, bf16[1,1,256,3584]{3,2,1,0:T(8,128)(2,1)}, bf16[1,1,256,3584]{3,2,1,0:T(8,128)(2,1)S(1)}) fusion(bf16[1,1,1024,3584]{3,2,1,0:T(8,128)(2,1)} %param.3), kind=kLoop, calls=%fused_computation.137 | loop fusion | bytes 14680064 | tf_op jit(solution)/shard_map/slice | solution.py:98
  15.6 3.8 copy.5
  26.0 3.8 copy.6
  32.2 3.8 copy.8
  62.9 5.6 %collective-permute-done.1 = f32[256,448]{0,1:T(8,128)S(1)} collective-permute-done((f32[256,448]{0,1:T(8,128)S(1)}, f32[256,448]{0,1:T(8,128)S(1)}, u32[]{:S(2)}, u32[]{:S(2)}) %collective-permute-start.1) | collective-permute-done | bytes 458784 | tf_op jit(solution)/shard_map/ppermute | solution.py:40
  72.2 9.3 %collective-permute-done.22 = f32[256,448]{0,1:T(8,128)S(1)} collective-permute-done((f32[256,448]{0,1:T(8,128)S(1)}, f32[256,448]{0,1:T(8,128)S(1)}, u32[]{:S(2)}, u32[]{:S(2)}) %collective-permute-start.22) | collective-permute-done | bytes 458784 | tf_op jit(solution)/shard_map/ppermute | solution.py:40
  83.7 4.4 collective-permute-done.2
  91.9 9.3 %collective-permute-done.23 = f32[256,448]{0,1:T(8,128)S(1)} collective-permute-done((f32[256,448]{0,1:T(8,128)S(1)}, f32[256,448]{0,1:T(8,128)S(1)}, u32[]{:S(2)}, u32[]{:S(2)}) %collective-permute-start.23) | collective-permute-done | bytes 458784 | tf_op jit(solution)/shard_map/ppermute | solution.py:40
  103.4 4.4 collective-permute-done.3
  111.5 9.3 %collective-permute-done.24 = f32[256,448]{0,1:T(8,128)S(1)} collective-permute-done((f32[256,448]{0,1:T(8,128)S(1)}, f32[256,448]{0,1:T(8,128)S(1)}, u32[]{:S(2)}, u32[]{:S(2)}) %collective-permute-start.24) | collective-permute-done | bytes 458784 | tf_op jit(solution)/shard_map/ppermute | solution.py:40
  123.0 4.4 collective-permute-done.4
  131.2 9.3 %collective-permute-done.25 = f32[256,448]{0,1:T(8,128)S(1)} collective-permute-done((f32[256,448]{0,1:T(8,128)S(1)}, f32[256,448]{0,1:T(8,128)S(1)}, u32[]{:S(2)}, u32[]{:S(2)}) %collective-permute-start.25) | collective-permute-done | bytes 458784 | tf_op jit(solution)/shard_map/ppermute | solution.py:40
  142.7 4.4 collective-permute-done.5
  150.9 9.3 %collective-permute-done.26 = f32[256,448]{0,1:T(8,128)S(1)} collective-permute-done((f32[256,448]{0,1:T(8,128)S(1)}, f32[256,448]{0,1:T(8,128)S(1)}, u32[]{:S(2)}, u32[]{:S(2)}) %collective-permute-start.26) | collective-permute-done | bytes 458784 | tf_op jit(solution)/shard_map/ppermute | solution.py:40
  162.4 4.4 collective-permute-done.6
  170.0 7.2 %collective-permute-done.27 = f32[256,448]{0,1:T(8,128)S(1)} collective-permute-done((f32[256,448]{0,1:T(8,128)S(1)}, f32[256,448]{0,1:T(8,128)S(1)}, u32[]{:S(2)}, u32[]{:S(2)}) %collective-permute-start.27) | collective-permute-done | bytes 458784 | tf_op jit(solution)/shard_map/ppermute | solution.py:40
  187.1 5.7 %collective-permute-done.28 = f32[1]{0:T(128)} collective-permute-done((f32[1]{0:T(128)}, f32[1]{0:T(128)}, u32[]{:S(2)}, u32[]{:S(2)}) %collective-permute-start.28) | collective-permute-done | bytes 36 | tf_op jit(solution)/shard_map/ppermute | solution.py:60
  194.1 4.2 collective-permute-done.29
  198.9 4.9 %collective-permute-done.30 = f32[1]{0:T(128)} collective-permute-done((f32[1]{0:T(128)}, f32[1]{0:T(128)}, u32[]{:S(2)}, u32[]{:S(2)}) %collective-permute-start.30) | collective-permute-done | bytes 36 | tf_op jit(solution)/shard_map/ppermute | solution.py:60
  222.2 105.2 %all-reduce.2.cloned.1.call-done = f32[512,1152]{0,1:T(8,128)} async-done(((f32[512,1152]{0,1:T(8,128)}), f32[512,1152]{0,1:T(8,128)}) %all-reduce.2.cloned.1.call-update) | async-done | bytes 2359312 | tf_op jit(solution)/shard_map/psum | solution.py:109
  376.2 10.9 %fusion.67 = f32[1024,1024]{0,1:T(8,128)S(1)} fusion(f32[1024,1024]{0,1:T(8,128)} %copy-done.11, f32[]{:T(128)S(6)} %mul.80), kind=kOutput, calls=%fused_computation.136 | convolution fusion | flops 6443499520 | bytes 8388612 | tf_op jit(solution)/shard_map/dot_general | solution.py:19
  387.1 7.0 %fusion.7 = f32[1024,448]{1,0:T(8,128)S(1)} fusion(f32[1024,1024]{0,1:T(8,128)S(1)} %fusion.67, f32[1,1024,448]{1,2,0:T(8,128)S(1)} %copy-done.18, f32[256,448]{0,1:T(8,128)S(1)} %copy-done.3, f32[256,448]{0,1:T(8,128)S(1)} %copy-done.5, f32[256,448]{0,1:T(8,128)S(1)} %convert_add_fusion.14, f32[256,448]{0,1:T(8,128)S(1)} %convert_add_fusion.21, ...), kind=kOutput, calls=%fused_computation.11 | convolution fusion | flops 2830041088 | bytes 13893644 | tf_op jit(solution)/shard_map/dot_general | solution.py:19
  394.1 13.8 %fusion.11 = f32[1024,1024]{1,0:T(8,128)S(1)} fusion(f32[1024,1024]{0,1:T(8,128)S(1)} %fusion.67, f32[1024,1024]{0,1:T(8,128)S(1)} %copy-done.12, f32[]{:T(128)S(6)} %mul.80), kind=kOutput, calls=%fused_computation.13 | convolution fusion | flops 6450839552 | bytes 12582916 | tf_op jit(solution)/shard_map/dot_general | solution.py:19
  407.9 8.7 %fusion.9 = f32[1024,1024]{1,0:T(8,128)} fusion(f32[1024,1024]{1,0:T(8,128)S(1)} %fusion.11, f32[1024,1024]{0,1:T(8,128)S(1)} %fusion.67, f32[1024,1024]{0,1:T(8,128)S(1)} %copy-done.12, f32[]{:T(128)S(6)} %mul.80), kind=kOutput, calls=%fused_computation.12 | convolution fusion | flops 6449790976 | bytes 16777220 | tf_op jit(solution)/shard_map/dot_general | solution.py:19
  416.5 5.4 %copy.38 = f32[1024,1024]{0,1:T(8,128)} copy(f32[1024,1024]{1,0:T(8,128)} %fusion.9) | data formatting | bytes 8388608 | tf_op jit(solution)/shard_map/dot_general | solution.py:19
  422.0 12.5 %fusion.1 = f32[1024,1024]{0,1:T(8,128)S(1)} fusion(f32[1024,1024]{0,1:T(8,128)} %copy.38, f32[1024,1024]{1,0:T(8,128)} %fusion.9), kind=kOutput, calls=%fused_computation.4 | convolution fusion | flops 6448742400 | bytes 12582912 | tf_op jit(solution)/shard_map/dot_general | solution.py:19
  434.5 7.0 %fusion.72 = f32[1024,1024]{1,0:T(8,128)S(1)} fusion(f32[1024,1024]{1,0:T(8,128)S(1)} %copy-done.15, f32[1024,1024]{0,1:T(8,128)S(1)} %fusion.1), kind=kOutput, calls=%fused_computation.141 | convolution fusion | flops 6442450944 | bytes 12582912 | tf_op jit(solution)/shard_map/dot_general | solution.py:19
  441.6 7.1 %fusion.73 = f32[1024,1024]{1,0:T(8,128)S(1)} fusion(f32[1024,1024]{1,0:T(8,128)S(1)} %fusion.72, f32[1024,1024]{0,1:T(8,128)S(1)} %fusion.1), kind=kOutput, calls=%fused_computation.142 | convolution fusion | flops 6442450944 | bytes 12582912 | tf_op jit(solution)/shard_map/dot_general | solution.py:19
  450.8 8.3 %fusion.74 = f32[1024,1024]{0,1:T(8,128)} fusion(f32[1024,1024]{1,0:T(8,128)S(1)} %fusion.73), kind=kOutput, calls=%fused_computation.143 | convolution fusion | flops 6442450944 | bytes 8388608 | tf_op jit(solution)/shard_map/dot_general | solution.py:19
  459.1 5.3 %copy.40 = f32[1024,1024]{0,1:T(8,128)} copy(f32[1024,1024]{1,0:T(8,128)} %copy-done.16) | data formatting | bytes 8388608 | tf_op jit(solution)/shard_map/dot_general | solution.py:19
  464.5 5.4 %fusion.75 = f32[1024,448]{1,0:T(8,128)S(1)} fusion(f32[1024,1024]{0,1:T(8,128)} %copy-done.14, f32[1024,448]{1,0:T(8,128)S(1)} %fusion.7), kind=kOutput, calls=%fused_computation.144 | convolution fusion | flops 2818572288 | bytes 7864320 | tf_op jit(solution)/shard_map/dot_general | solution.py:19
  469.9 4.5 multiply_bitcast_fusion
  (256 shorter events, 130.0 us)
Async XLA Ops:
  7.2 320.2 %all-reduce.2.cloned.1.call-start = ((), (), s32[]{:S(2)}) async-start(), calls=%async_computation | async-start | bytes 4718592 | tf_op jit(solution)/shard_map/psum | solution.py:109
  21.8 32.0 %collective-permute-start = (f32[256,448]{0,1:T(8,128)}, f32[256,448]{0,1:T(8,128)S(1)}, u32[]{:S(2)}, u32[]{:S(2)}) collective-permute-start(f32[256,448]{0,1:T(8,128)} %bitcast_convert_fusion.3), channel_id=1, source_target_pairs={{0,8},{8,16},{16,24},{24,28},{28,20},{20,12},{12,4},{4,0},{1,9},{9... | collective-permute-start | bytes 1376264 | tf_op jit(solution)/shard_map/ppermute | solution.py:40
  32.2 24.8 %collective-permute-start.7 = (f32[256,448]{0,1:T(8,128)}, f32[256,448]{0,1:T(8,128)}, u32[]{:S(2)}, u32[]{:S(2)}) collective-permute-start(f32[256,448]{0,1:T(8,128)} %bitcast_convert_fusion.2), channel_id=1, source_target_pairs={{0,4},{8,0},{16,8},{24,16},{28,24},{20,28},{12,20},{4,12},{1,5},{9... | collective-permute-start | bytes 1376264 | tf_op jit(solution)/shard_map/ppermute | solution.py:40
  37.7 20.9 %collective-permute-start.21 = (f32[256,448]{0,1:T(8,128)}, f32[256,448]{0,1:T(8,128)}, u32[]{:S(2)}, u32[]{:S(2)}) collective-permute-start(f32[256,448]{0,1:T(8,128)} %bitcast_convert_fusion), channel_id=1, source_target_pairs={{0,4},{8,0},{16,8},{24,16},{28,24},{20,28},{12,20},{4,12},{1,5},{9... | collective-permute-start | bytes 1376264 | tf_op jit(solution)/shard_map/ppermute | solution.py:40
  43.0 18.4 %collective-permute-start.14 = (f32[256,448]{0,1:T(8,128)S(1)}, f32[256,448]{0,1:T(8,128)S(1)}, u32[]{:S(2)}, u32[]{:S(2)}) collective-permute-start(f32[256,448]{0,1:T(8,128)S(1)} %bitcast_convert_fusion.1), channel_id=1, source_target_pairs={{0,8},{8,16},{16,24},{24,28},{28,20},{20,12},{12,4},{4,0},{1,9},{9... | collective-permute-start | bytes 1376264 | tf_op jit(solution)/shard_map/ppermute | solution.py:40
  54.9 13.5 %collective-permute-start.1 = (f32[256,448]{0,1:T(8,128)S(1)}, f32[256,448]{0,1:T(8,128)S(1)}, u32[]{:S(2)}, u32[]{:S(2)}) collective-permute-start(f32[256,448]{0,1:T(8,128)S(1)} %convert_add_fusion.27), channel_id=1, source_target_pairs={{0,8},{8,16},{16,24},{24,28},{28,20},{20,12},{12,4},{4,0},{1,9},{9... | collective-permute-start | bytes 1376264 | tf_op jit(solution)/shard_map/ppermute | solution.py:40
  59.8 21.7 %collective-permute-start.22 = (f32[256,448]{0,1:T(8,128)S(1)}, f32[256,448]{0,1:T(8,128)S(1)}, u32[]{:S(2)}, u32[]{:S(2)}) collective-permute-start(f32[256,448]{0,1:T(8,128)S(1)} %convert_add_fusion.6), channel_id=1, source_target_pairs={{0,4},{8,0},{16,8},{24,16},{28,24},{20,28},{12,20},{4,12},{1,5},{9... | collective-permute-start | bytes 1376264 | tf_op jit(solution)/shard_map/ppermute | solution.py:40
  62.4 19.7 %collective-permute-start.15 = (f32[256,448]{0,1:T(8,128)S(1)}, f32[256,448]{0,1:T(8,128)S(1)}, u32[]{:S(2)}, u32[]{:S(2)}) collective-permute-start(f32[256,448]{0,1:T(8,128)S(1)} %convert_add_fusion.13), channel_id=1, source_target_pairs={{0,8},{8,16},{16,24},{24,28},{28,20},{20,12},{12,4},{4,0},{1,9},{9... | collective-permute-start | bytes 1376264 | tf_op jit(solution)/shard_map/ppermute | solution.py:40
  68.5 19.6 %collective-permute-start.2 = (f32[256,448]{0,1:T(8,128)S(1)}, f32[256,448]{0,1:T(8,128)S(1)}, u32[]{:S(2)}, u32[]{:S(2)}) collective-permute-start(f32[256,448]{0,1:T(8,128)S(1)} %convert_add_fusion.26), channel_id=1, source_target_pairs={{0,8},{8,16},{16,24},{24,28},{28,20},{20,12},{12,4},{4,0},{1,9},{9... | collective-permute-start | bytes 1376264 | tf_op jit(solution)/shard_map/ppermute | solution.py:40
  71.7 19.6 %collective-permute-start.9 = (f32[256,448]{0,1:T(8,128)S(1)}, f32[256,448]{0,1:T(8,128)S(1)}, u32[]{:S(2)}, u32[]{:S(2)}) collective-permute-start(f32[256,448]{0,1:T(8,128)S(1)} %convert_add_fusion.19), channel_id=1, source_target_pairs={{0,4},{8,0},{16,8},{24,16},{28,24},{20,28},{12,20},{4,12},{1,5},{9... | collective-permute-start | bytes 1376264 | tf_op jit(solution)/shard_map/ppermute | solution.py:40
  81.5 19.6 %collective-permute-start.23 = (f32[256,448]{0,1:T(8,128)S(1)}, f32[256,448]{0,1:T(8,128)S(1)}, u32[]{:S(2)}, u32[]{:S(2)}) collective-permute-start(f32[256,448]{0,1:T(8,128)S(1)} %convert_add_fusion.5), channel_id=1, source_target_pairs={{0,4},{8,0},{16,8},{24,16},{28,24},{20,28},{12,20},{4,12},{1,5},{9... | collective-permute-start | bytes 1376264 | tf_op jit(solution)/shard_map/ppermute | solution.py:40
  82.1 19.6 %collective-permute-start.16 = (f32[256,448]{0,1:T(8,128)S(1)}, f32[256,448]{0,1:T(8,128)S(1)}, u32[]{:S(2)}, u32[]{:S(2)}) collective-permute-start(f32[256,448]{0,1:T(8,128)S(1)} %convert_add_fusion.12), channel_id=1, source_target_pairs={{0,8},{8,16},{16,24},{24,28},{28,20},{20,12},{12,4},{4,0},{1,9},{9... | collective-permute-start | bytes 1376264 | tf_op jit(solution)/shard_map/ppermute | solution.py:40
  88.2 19.6 %collective-permute-start.3 = (f32[256,448]{0,1:T(8,128)S(1)}, f32[256,448]{0,1:T(8,128)S(1)}, u32[]{:S(2)}, u32[]{:S(2)}) collective-permute-start(f32[256,448]{0,1:T(8,128)S(1)} %convert_add_fusion.25), channel_id=1, source_target_pairs={{0,8},{8,16},{16,24},{24,28},{28,20},{20,12},{12,4},{4,0},{1,9},{9... | collective-permute-start | bytes 1376264 | tf_op jit(solution)/shard_map/ppermute | solution.py:40
  91.4 19.6 %collective-permute-start.10 = (f32[256,448]{0,1:T(8,128)S(1)}, f32[256,448]{0,1:T(8,128)S(1)}, u32[]{:S(2)}, u32[]{:S(2)}) collective-permute-start(f32[256,448]{0,1:T(8,128)S(1)} %convert_add_fusion.18), channel_id=1, source_target_pairs={{0,4},{8,0},{16,8},{24,16},{28,24},{20,28},{12,20},{4,12},{1,5},{9... | collective-permute-start | bytes 1376264 | tf_op jit(solution)/shard_map/ppermute | solution.py:40
  101.2 19.6 %collective-permute-start.24 = (f32[256,448]{0,1:T(8,128)S(1)}, f32[256,448]{0,1:T(8,128)S(1)}, u32[]{:S(2)}, u32[]{:S(2)}) collective-permute-start(f32[256,448]{0,1:T(8,128)S(1)} %convert_add_fusion.4), channel_id=1, source_target_pairs={{0,4},{8,0},{16,8},{24,16},{28,24},{20,28},{12,20},{4,12},{1,5},{9... | collective-permute-start | bytes 1376264 | tf_op jit(solution)/shard_map/ppermute | solution.py:40
  101.8 19.6 %collective-permute-start.17 = (f32[256,448]{0,1:T(8,128)S(1)}, f32[256,448]{0,1:T(8,128)S(1)}, u32[]{:S(2)}, u32[]{:S(2)}) collective-permute-start(f32[256,448]{0,1:T(8,128)S(1)} %convert_add_fusion.11), channel_id=1, source_target_pairs={{0,8},{8,16},{16,24},{24,28},{28,20},{20,12},{12,4},{4,0},{1,9},{9... | collective-permute-start | bytes 1376264 | tf_op jit(solution)/shard_map/ppermute | solution.py:40
  107.8 19.6 %collective-permute-start.4 = (f32[256,448]{0,1:T(8,128)S(1)}, f32[256,448]{0,1:T(8,128)S(1)}, u32[]{:S(2)}, u32[]{:S(2)}) collective-permute-start(f32[256,448]{0,1:T(8,128)S(1)} %convert_add_fusion.24), channel_id=1, source_target_pairs={{0,8},{8,16},{16,24},{24,28},{28,20},{20,12},{12,4},{4,0},{1,9},{9... | collective-permute-start | bytes 1376264 | tf_op jit(solution)/shard_map/ppermute | solution.py:40
  111.0 19.6 %collective-permute-start.11 = (f32[256,448]{0,1:T(8,128)S(1)}, f32[256,448]{0,1:T(8,128)S(1)}, u32[]{:S(2)}, u32[]{:S(2)}) collective-permute-start(f32[256,448]{0,1:T(8,128)S(1)} %convert_add_fusion.17), channel_id=1, source_target_pairs={{0,4},{8,0},{16,8},{24,16},{28,24},{20,28},{12,20},{4,12},{1,5},{9... | collective-permute-start | bytes 1376264 | tf_op jit(solution)/shard_map/ppermute | solution.py:40
  120.9 19.6 %collective-permute-start.25 = (f32[256,448]{0,1:T(8,128)S(1)}, f32[256,448]{0,1:T(8,128)S(1)}, u32[]{:S(2)}, u32[]{:S(2)}) collective-permute-start(f32[256,448]{0,1:T(8,128)S(1)} %convert_add_fusion.3), channel_id=1, source_target_pairs={{0,4},{8,0},{16,8},{24,16},{28,24},{20,28},{12,20},{4,12},{1,5},{9... | collective-permute-start | bytes 1376264 | tf_op jit(solution)/shard_map/ppermute | solution.py:40
  121.4 19.6 %collective-permute-start.18 = (f32[256,448]{0,1:T(8,128)S(1)}, f32[256,448]{0,1:T(8,128)S(1)}, u32[]{:S(2)}, u32[]{:S(2)}) collective-permute-start(f32[256,448]{0,1:T(8,128)S(1)} %convert_add_fusion.10), channel_id=1, source_target_pairs={{0,8},{8,16},{16,24},{24,28},{28,20},{20,12},{12,4},{4,0},{1,9},{9... | collective-permute-start | bytes 1376264 | tf_op jit(solution)/shard_map/ppermute | solution.py:40
  127.5 19.6 %collective-permute-start.5 = (f32[256,448]{0,1:T(8,128)S(1)}, f32[256,448]{0,1:T(8,128)S(1)}, u32[]{:S(2)}, u32[]{:S(2)}) collective-permute-start(f32[256,448]{0,1:T(8,128)S(1)} %convert_add_fusion.23), channel_id=1, source_target_pairs={{0,8},{8,16},{16,24},{24,28},{28,20},{20,12},{12,4},{4,0},{1,9},{9... | collective-permute-start | bytes 1376264 | tf_op jit(solution)/shard_map/ppermute | solution.py:40
  130.7 19.6 %collective-permute-start.12 = (f32[256,448]{0,1:T(8,128)S(1)}, f32[256,448]{0,1:T(8,128)S(1)}, u32[]{:S(2)}, u32[]{:S(2)}) collective-permute-start(f32[256,448]{0,1:T(8,128)S(1)} %convert_add_fusion.16), channel_id=1, source_target_pairs={{0,4},{8,0},{16,8},{24,16},{28,24},{20,28},{12,20},{4,12},{1,5},{9... | collective-permute-start | bytes 1376264 | tf_op jit(solution)/shard_map/ppermute | solution.py:40
  140.5 19.6 %collective-permute-start.26 = (f32[256,448]{0,1:T(8,128)S(1)}, f32[256,448]{0,1:T(8,128)S(1)}, u32[]{:S(2)}, u32[]{:S(2)}) collective-permute-start(f32[256,448]{0,1:T(8,128)S(1)} %convert_add_fusion.2), channel_id=1, source_target_pairs={{0,4},{8,0},{16,8},{24,16},{28,24},{20,28},{12,20},{4,12},{1,5},{9... | collective-permute-start | bytes 1376264 | tf_op jit(solution)/shard_map/ppermute | solution.py:40
  141.1 19.6 %collective-permute-start.19 = (f32[256,448]{0,1:T(8,128)S(1)}, f32[256,448]{0,1:T(8,128)S(1)}, u32[]{:S(2)}, u32[]{:S(2)}) collective-permute-start(f32[256,448]{0,1:T(8,128)S(1)} %convert_add_fusion.9), channel_id=1, source_target_pairs={{0,8},{8,16},{16,24},{24,28},{28,20},{20,12},{12,4},{4,0},{1,9},{9... | collective-permute-start | bytes 1376264 | tf_op jit(solution)/shard_map/ppermute | solution.py:40
  147.2 19.6 %collective-permute-start.6 = (f32[256,448]{0,1:T(8,128)S(1)}, f32[256,448]{0,1:T(8,128)S(1)}, u32[]{:S(2)}, u32[]{:S(2)}) collective-permute-start(f32[256,448]{0,1:T(8,128)S(1)} %convert_add_fusion.22), channel_id=1, source_target_pairs={{0,8},{8,16},{16,24},{24,28},{28,20},{20,12},{12,4},{4,0},{1,9},{9... | collective-permute-start | bytes 1376264 | tf_op jit(solution)/shard_map/ppermute | solution.py:40
  150.4 19.6 %collective-permute-start.13 = (f32[256,448]{0,1:T(8,128)S(1)}, f32[256,448]{0,1:T(8,128)S(1)}, u32[]{:S(2)}, u32[]{:S(2)}) collective-permute-start(f32[256,448]{0,1:T(8,128)S(1)} %convert_add_fusion.15), channel_id=1, source_target_pairs={{0,4},{8,0},{16,8},{24,16},{28,24},{20,28},{12,20},{4,12},{1,5},{9... | collective-permute-start | bytes 1376264 | tf_op jit(solution)/shard_map/ppermute | solution.py:40
  160.2 17.0 %collective-permute-start.27 = (f32[256,448]{0,1:T(8,128)S(1)}, f32[256,448]{0,1:T(8,128)S(1)}, u32[]{:S(2)}, u32[]{:S(2)}) collective-permute-start(f32[256,448]{0,1:T(8,128)S(1)} %convert_add_fusion.1), channel_id=1, source_target_pairs={{0,4},{8,0},{16,8},{24,16},{28,24},{20,28},{12,20},{4,12},{1,5},{9... | collective-permute-start | bytes 1376264 | tf_op jit(solution)/shard_map/ppermute | solution.py:40
  160.7 16.5 %collective-permute-start.20 = (f32[256,448]{0,1:T(8,128)S(1)}, f32[256,448]{0,1:T(8,128)S(1)}, u32[]{:S(2)}, u32[]{:S(2)}) collective-permute-start(f32[256,448]{0,1:T(8,128)S(1)} %convert_add_fusion.8), channel_id=1, source_target_pairs={{0,8},{8,16},{16,24},{24,28},{28,20},{20,12},{12,4},{4,0},{1,9},{9... | collective-permute-start | bytes 1376264 | tf_op jit(solution)/shard_map/ppermute | solution.py:40
  178.4 28.0 %collective-permute-start.34 = (f32[1]{0:T(128)}, f32[1]{0:T(128)}, u32[]{:S(2)}, u32[]{:S(2)}) collective-permute-start(f32[1]{0:T(128)} %bitcast.44), channel_id=1, source_target_pairs={{0,28},{4,0},{8,4},{12,8},{16,12},{20,16},{24,20},{28,24},{1,29},{... | collective-permute-start | bytes 20 | tf_op jit(solution)/shard_map/ppermute | solution.py:60
  182.2 23.5 %collective-permute-start.33 = (f32[1]{0:T(128)}, f32[1]{0:T(128)}, u32[]{:S(2)}, u32[]{:S(2)}) collective-permute-start(f32[1]{0:T(128)} %bitcast.44), channel_id=1, source_target_pairs={{0,24},{4,28},{8,0},{12,4},{16,8},{20,12},{24,16},{28,20},{1,25},{... | collective-permute-start | bytes 20 | tf_op jit(solution)/shard_map/ppermute | solution.py:60
  182.6 22.4 %collective-permute-start.32 = (f32[1]{0:T(128)}, f32[1]{0:T(128)}, u32[]{:S(2)}, u32[]{:S(2)}) collective-permute-start(f32[1]{0:T(128)} %bitcast.44), channel_id=1, source_target_pairs={{0,20},{4,24},{8,28},{12,0},{16,4},{20,8},{24,12},{28,16},{1,21},{... | collective-permute-start | bytes 20 | tf_op jit(solution)/shard_map/ppermute | solution.py:60
  182.9 21.5 %collective-permute-start.31 = (f32[1]{0:T(128)}, f32[1]{0:T(128)}, u32[]{:S(2)}, u32[]{:S(2)}) collective-permute-start(f32[1]{0:T(128)} %bitcast.44), channel_id=1, source_target_pairs={{0,16},{4,20},{8,24},{12,28},{16,0},{20,4},{24,8},{28,12},{1,17},{... | collective-permute-start | bytes 20 | tf_op jit(solution)/shard_map/ppermute | solution.py:60
  (48 other events, 480.8 us)
Sparse Core Ops, SparseCore 0:
  222.4 104.9 all-reduce.1
